TPU v7x, 32 devices: a whole 2x2x4 slice. The times are simulated.
32 devices in a mesh: section: 4 (over y, x), dp: 8 (over z, core).
Axes of the slice: x: 2, y: 2, z: 4, core: 2. Of those that a mesh axis runs over, the one named last changes fastest.
Arguments:
- patches: bfloat16 [2, 5120, 768], P(None, 'dp'), may hold values from -6 to 6
- positions: bfloat16 [878, 768], replicated, may hold values from -3 to 3
- image_sizes: int32 [2, 8, 6], P(None, 'dp'), may hold values from 0 to 3, as said below
- keep_masks: int32 [2, 8, 6, 4], P(None, 'dp'), may hold values 0 or 1
- output_grad: bfloat16 [2, 5120, 768], P(None, 'dp'), may hold values from -6 to 6
- vector_params: float32 [2, 12, 768], P(None, None, 'dp'), may hold values from -0.9 to 1.6, as said below
- attention_weights: float32 [2, 768, 3072], P(None, 'dp'), may hold values from -0.8660254 to 0.8660254
- feedforward_weights: float32 [2, 2, 768, 3072], P(None, None, 'dp'), may hold values from -0.108253175 to 0.108253175
- vector_first: float32 [2, 12, 768], P(None, None, 'dp'), may hold values from -6 to 6
- attention_first: float32 [2, 768, 3072], P(None, 'dp'), may hold values from -6 to 6
- feedforward_first: float32 [2, 2, 768, 3072], P(None, None, 'dp'), may hold values from -6 to 6
- vector_second: float32 [2, 12, 768], P(None, None, 'dp'), may hold values from 1 to 100
- attention_second: float32 [2, 768, 3072], P(None, 'dp'), may hold values from 1 to 100
- feedforward_second: float32 [2, 2, 768, 3072], P(None, None, 'dp'), may hold values from 1 to 100
- layer_rates: float32 [2], replicated, may hold values from 0.4 to 1
Outputs:
- block_out: bfloat16 [2, 5120, 768], P(None, 'dp', 'section')
- input_grad: float32 [2, 5120, 768], P(None, 'dp', 'section')
- vector_grad: float32 [2, 12, 768], P(None, None, 'dp')
- attention_grad: float32 [2, 768, 3072], P(None, 'dp')
- feedforward_grad: float32 [2, 2, 768, 3072], P(None, None, 'dp')
- vector_mean: float32 [2, 12, 768], P(None, None, 'dp')
- attention_mean: float32 [2, 768, 3072], P(None, 'dp')
- feedforward_mean: float32 [2, 2, 768, 3072], P(None, None, 'dp')
- vector_square: float32 [2, 12, 768], P(None, None, 'dp')
- attention_square: float32 [2, 768, 3072], P(None, 'dp')
- feedforward_square: float32 [2, 2, 768, 3072], P(None, None, 'dp')
- vector_step: float32 [2, 12, 768], P(None, None, 'dp')
- attention_step: float32 [2, 768, 3072], P(None, 'dp')
- feedforward_step: float32 [2, 2, 768, 3072], P(None, None, 'dp')
Inputs may be any that keep to these rules, and one draw needn't show every extreme that they name: `image_sizes`: 3 marks an empty slot. The images of the used slots, in slot order, fill the first rows of their unit and fit within its 640 rows; the rest of the unit is padding. `vector_params`: rows 0 and 5 lie near 1, the others near 0.
All inputs are finite; a program needn't handle non-finite values. No bound on the sum of `keep_masks` on one device may be relied on, other than what follows from the above.
Results may differ from a plain program's by a relative error of at most 0.015.
The roundings to bfloat16 on the way count: a program that leaves them out, or rounds other values in their place, can miss the bound.
Values may be sent and summed in bfloat16 or wider, within the bound.
No kernel may reach another device: no remote copies, remote signals or barrier semaphores. Data moves between devices by JAX's collectives and lax.ppermute only.
A program may use at most 384 MiB of HBM per device.

v0:
```python
import jax
import jax.numpy as jnp
from jax import lax
from jax.sharding import PartitionSpec as P

H = 12
HD = 64
GRID_S = 10
GRID_M = 14
GRID_L = 24


beta_one = 0.9
beta_two = 0.999
bias_one = 1.0 - 0.9**10
bias_two = 1.0 - 0.999**10
adam_eps = 1e-08
decay_rate = 0.05
drop_rate = 0.1
norm_eps = 1e-06
masked_score = -1e30
root_half = 0.7071067811865476
normal_peak = 0.3989422804014327


def shortened(array):

    def short(part):
        return part.astype(jnp.bfloat16) if part.dtype == jnp.float32 else part

    return jax.tree.map(short, array)


def passed_along(value, axis, steps):
    count = lax.axis_size(axis)
    initial, last = (max(0, -steps), min(count, count - steps))
    return lax.ppermute(value, axis, [(source, source + steps) for source in range(initial, last)])


def image_layout(image_ids, row_count):
    small_len = GRID_S * GRID_S + 2
    middle_len = GRID_M * GRID_M + 2
    large_len = GRID_L * GRID_L + 2
    lengths = jnp.where(
        image_ids == 0,
        small_len,
        jnp.where(image_ids == 1, middle_len, jnp.where(image_ids == 2, large_len, 0)),
    ).astype(jnp.int32)
    slot_ends = jnp.cumsum(lengths)
    slot_starts = slot_ends - lengths
    row_index = jnp.arange(row_count, dtype=jnp.int32)
    segment = jnp.sum((row_index[:, None] >= slot_ends[None, :]).astype(jnp.int32), axis=1)
    member = segment[:, None] == jnp.arange(image_ids.shape[0], dtype=jnp.int32)[None, :]
    first_row = jnp.sum(jnp.where(member, slot_starts[None, :], 0), axis=1)
    kind_row = jnp.sum(jnp.where(member, image_ids[None, :], 0), axis=1)
    table_start = jnp.where(
        kind_row == 0, 0, jnp.where(kind_row == 1, small_len, small_len + middle_len)
    ).astype(jnp.int32)
    in_image = segment < image_ids.shape[0]
    table_row = jnp.where(in_image, table_start + row_index - first_row, 0)
    return (segment, member, in_image, table_row)


def normalize(hidden, gain, shift):
    center = hidden - jnp.mean(hidden, axis=-1, keepdims=True)
    inverse = lax.rsqrt(jnp.mean(center * center, axis=-1, keepdims=True) + norm_eps)
    scaled = center * inverse
    return (scaled * gain + shift, scaled, inverse)


def normalize_back(normed_grad, scaled, inverse, gain):
    scaled_grad = normed_grad * gain
    centered = scaled_grad - jnp.mean(scaled_grad, axis=-1, keepdims=True)
    return inverse * (centered - scaled * jnp.mean(scaled_grad * scaled, axis=-1, keepdims=True))


def attention_parts(hidden, vector_rows, attn_mats, same_image):
    row_count = hidden.shape[0]
    feature_count = hidden.shape[1]
    normed, scaled, inverse = normalize(
        hidden, vector_rows[0].astype(jnp.float32), vector_rows[1].astype(jnp.float32)
    )
    normed_low = normed.astype(jnp.bfloat16)
    joined_bias = jnp.concatenate(
        [vector_rows[2], jnp.zeros_like(vector_rows[2]), vector_rows[3]]
    ).astype(jnp.float32)
    joined = jnp.dot(
        normed_low, attn_mats[:, : 3 * feature_count], preferred_element_type=jnp.float32
    )
    joined = (joined + joined_bias).astype(jnp.bfloat16)
    query_rows = joined[:, :feature_count].reshape(row_count, H, HD)
    key_rows = joined[:, feature_count : 2 * feature_count].reshape(row_count, H, HD)
    value_rows = joined[:, 2 * feature_count :].reshape(row_count, H, HD)
    scores = jnp.einsum(
        "qhd,khd->hqk", query_rows, key_rows, preferred_element_type=jnp.float32
    ) * HD ** (-0.5)
    scores = jnp.where(same_image[None], scores, masked_score)
    row_peak = jnp.max(scores, axis=-1, keepdims=True)
    exp_scores = jnp.exp(scores - row_peak)
    softmax_out = exp_scores / jnp.sum(exp_scores, axis=-1, keepdims=True)
    softmax_low = softmax_out.astype(jnp.bfloat16)
    mixed = jnp.einsum("hqk,khd->qhd", softmax_low, value_rows, preferred_element_type=jnp.float32)
    mixed = mixed.astype(jnp.bfloat16).reshape(row_count, feature_count)
    return (
        normed_low,
        scaled,
        inverse,
        query_rows,
        key_rows,
        value_rows,
        softmax_out,
        softmax_low,
        mixed,
    )


def attention_forward(hidden, vector_rows, attn_mats, factor, same_image):
    feature_count = hidden.shape[1]
    mixed = attention_parts(hidden, vector_rows, attn_mats, same_image)[8]
    branch = jnp.dot(mixed, attn_mats[:, 3 * feature_count :], preferred_element_type=jnp.float32)
    branch = branch + vector_rows[4].astype(jnp.float32)
    return (hidden + factor[:, None] * branch).astype(jnp.bfloat16)


def attention_backward(hidden, upstream, vector_rows, attn_mats, factor, same_image):
    row_count = hidden.shape[0]
    feature_count = hidden.shape[1]
    (
        normed_low,
        scaled,
        inverse,
        query_rows,
        key_rows,
        value_rows,
        softmax_out,
        softmax_low,
        mixed,
    ) = attention_parts(hidden, vector_rows, attn_mats, same_image)
    score_scale = HD ** (-0.5)
    branch_grad = (factor[:, None] * upstream).astype(jnp.bfloat16)
    out_weight_grad = jnp.einsum(
        "rd,re->de", mixed, branch_grad, preferred_element_type=jnp.float32
    )
    out_bias_grad = jnp.sum(branch_grad.astype(jnp.float32), axis=0)
    mixed_grad = jnp.einsum(
        "re,de->rd",
        branch_grad,
        attn_mats[:, 3 * feature_count :],
        preferred_element_type=jnp.float32,
    )
    mixed_grad = mixed_grad.astype(jnp.bfloat16).reshape(row_count, H, HD)
    value_grad = jnp.einsum(
        "hqk,qhd->khd", softmax_low, mixed_grad, preferred_element_type=jnp.float32
    )
    prob_grad = jnp.einsum(
        "qhd,khd->hqk", mixed_grad, value_rows, preferred_element_type=jnp.float32
    )
    score_grad = softmax_out * (
        prob_grad - jnp.sum(softmax_out * prob_grad, axis=-1, keepdims=True)
    )
    score_grad = score_grad.astype(jnp.bfloat16)
    query_grad = (
        jnp.einsum("hqk,khd->qhd", score_grad, key_rows, preferred_element_type=jnp.float32)
        * score_scale
    )
    key_grad = (
        jnp.einsum("hqk,qhd->khd", score_grad, query_rows, preferred_element_type=jnp.float32)
        * score_scale
    )
    joined_grad = jnp.concatenate(
        [
            query_grad.reshape(row_count, feature_count),
            key_grad.reshape(row_count, feature_count),
            value_grad.reshape(row_count, feature_count),
        ],
        axis=1,
    ).astype(jnp.bfloat16)
    in_weight_grad = jnp.einsum(
        "rd,re->de", normed_low, joined_grad, preferred_element_type=jnp.float32
    )
    joined_sums = jnp.sum(joined_grad.astype(jnp.float32), axis=0)
    normed_grad = jnp.einsum(
        "re,de->rd",
        joined_grad,
        attn_mats[:, : 3 * feature_count],
        preferred_element_type=jnp.float32,
    )
    hidden_grad = upstream + normalize_back(
        normed_grad, scaled, inverse, vector_rows[0].astype(jnp.float32)
    )
    zero_row = jnp.zeros((feature_count,), jnp.float32)
    vector_grad = jnp.stack(
        [
            jnp.sum(normed_grad * scaled, axis=0),
            jnp.sum(normed_grad, axis=0),
            joined_sums[:feature_count],
            joined_sums[2 * feature_count :],
            out_bias_grad,
        ]
        + [zero_row] * (vector_rows.shape[0] - 5)
    )
    attention_grad = jnp.concatenate([in_weight_grad, out_weight_grad], axis=1)
    return (hidden_grad, vector_grad, attention_grad)


def feedforward_parts(hidden, vector_rows, ff_mats):
    normed, scaled, inverse = normalize(
        hidden, vector_rows[5].astype(jnp.float32), vector_rows[6].astype(jnp.float32)
    )
    normed_low = normed.astype(jnp.bfloat16)
    inner = jnp.dot(normed_low, ff_mats[0], preferred_element_type=jnp.float32) + vector_rows[
        8:
    ].reshape(-1).astype(jnp.float32)
    activated = (0.5 * inner * (1.0 + lax.erf(inner * root_half))).astype(jnp.bfloat16)
    return (normed_low, scaled, inverse, inner, activated)


def feedforward_forward(hidden, vector_rows, ff_mats, factor):
    activated = feedforward_parts(hidden, vector_rows, ff_mats)[4]
    branch = jnp.einsum("rf,df->rd", activated, ff_mats[1], preferred_element_type=jnp.float32)
    branch = branch + vector_rows[7].astype(jnp.float32)
    return (hidden + factor[:, None] * branch).astype(jnp.bfloat16)


def feedforward_backward(hidden, upstream, vector_rows, ff_mats, factor):
    feature_count = hidden.shape[1]
    normed_low, scaled, inverse, inner, activated = feedforward_parts(hidden, vector_rows, ff_mats)
    branch_grad = (factor[:, None] * upstream).astype(jnp.bfloat16)
    second_bias_grad = jnp.sum(branch_grad.astype(jnp.float32), axis=0)
    second_weight_grad = jnp.einsum(
        "rd,rf->df", branch_grad, activated, preferred_element_type=jnp.float32
    )
    activated_grad = jnp.einsum(
        "rd,df->rf", branch_grad, ff_mats[1], preferred_element_type=jnp.float32
    )
    normal_cdf = 0.5 * (1.0 + lax.erf(inner * root_half))
    slope = normal_cdf + inner * jnp.exp(-0.5 * inner * inner) * normal_peak
    inner_grad = (activated_grad * slope).astype(jnp.bfloat16)
    first_weight_grad = jnp.einsum(
        "rd,rf->df", normed_low, inner_grad, preferred_element_type=jnp.float32
    )
    first_bias_grad = jnp.sum(inner_grad.astype(jnp.float32), axis=0)
    normed_grad = jnp.einsum(
        "rf,df->rd", inner_grad, ff_mats[0], preferred_element_type=jnp.float32
    )
    hidden_grad = upstream + normalize_back(
        normed_grad, scaled, inverse, vector_rows[5].astype(jnp.float32)
    )
    zero_row = jnp.zeros((feature_count,), jnp.float32)
    head_rows = jnp.stack(
        [zero_row] * 5
        + [jnp.sum(normed_grad * scaled, axis=0), jnp.sum(normed_grad, axis=0), second_bias_grad]
    )
    vector_grad = jnp.concatenate([head_rows, first_bias_grad.reshape(-1, feature_count)], axis=0)
    feedforward_grad = jnp.stack([first_weight_grad, second_weight_grad])
    return (hidden_grad, vector_grad, feedforward_grad)


def place_layer(piece, layer_id, layer_total):
    holder = jnp.zeros((layer_total,) + piece.shape, jnp.float32)
    return lax.dynamic_update_index_in_dim(holder, piece, layer_id, 0)


def adam_update(weight, first_moment, second_moment, gradient, layer_rates, decay_on):
    layer_rate = layer_rates.reshape((-1,) + (1,) * (weight.ndim - 1))
    mean_next = beta_one * first_moment + (1.0 - beta_one) * gradient
    square_next = beta_two * second_moment + (1.0 - beta_two) * gradient * gradient
    step_next = layer_rate * (
        mean_next / bias_one / (jnp.sqrt(square_next / bias_two) + adam_eps) + decay_on * weight
    )
    return (mean_next, square_next, step_next)


def shards(
    patches,
    positions,
    image_sizes,
    keep_masks,
    output_grad,
    vector_params,
    attention_weights,
    feedforward_weights,
    vector_first,
    attention_first,
    feedforward_first,
    vector_second,
    attention_second,
    feedforward_second,
    layer_rates,
):
    sections = lax.axis_size("section")
    micro_count = patches.shape[0]
    row_count = patches.shape[1]
    feature_count = patches.shape[2]
    layer_total = vector_params.shape[0]
    section_id = lax.axis_index("section")
    layer_id = section_id // 2
    section_kind = section_id % 2
    clocks = micro_count + sections - 1

    def own_layer(param):
        return lax.dynamic_index_in_dim(param, layer_id, 0, keepdims=False).astype(jnp.bfloat16)

    local_vectors = own_layer(vector_params)
    local_attention = own_layer(attention_weights)
    local_feedforward = own_layer(feedforward_weights)
    forward_weights = (
        lax.all_gather(local_vectors, "dp", axis=1, tiled=True),
        lax.all_gather(local_attention, "dp", axis=0, tiled=True),
        lax.all_gather(local_feedforward, "dp", axis=1, tiled=True),
    )
    segment_all, member_all, inside_all, table_all = jax.vmap(
        lambda image_ids: image_layout(image_ids, row_count)
    )(image_sizes[:, 0])
    keep_column = lax.dynamic_index_in_dim(keep_masks[:, 0], section_id, 2, keepdims=False)
    kept = jnp.sum(jnp.where(member_all, keep_column[:, None, :], 0), axis=2).astype(jnp.float32)
    factor_all = jnp.where(inside_all, kept / (1.0 - drop_rate), 1.0)
    position_rows = jnp.take(positions, table_all, axis=0).astype(jnp.float32)
    inputs_all = patches.astype(jnp.float32) + jnp.where(inside_all[:, :, None], position_rows, 0.0)

    def spare_forward(hidden, factor, same_image):
        return jnp.zeros((row_count, feature_count), jnp.bfloat16)

    def attention_run(hidden, factor, same_image):
        return attention_forward(hidden, forward_weights[0], forward_weights[1], factor, same_image)

    def feedforward_run(hidden, factor, same_image):
        return feedforward_forward(hidden, forward_weights[0], forward_weights[2], factor)

    stash = jnp.zeros((micro_count, row_count, feature_count), jnp.float32)
    block_all = jnp.zeros((micro_count, row_count, feature_count), jnp.float32)
    incoming = jnp.zeros((row_count, feature_count), jnp.bfloat16)
    for clock_tick in range(clocks):
        position = clock_tick - section_id
        active = (position >= 0) & (position < micro_count)
        micro_slot = jnp.clip(position, 0, micro_count - 1)
        hidden = jnp.where(section_id == 0, inputs_all[micro_slot], incoming.astype(jnp.float32))
        segment = segment_all[micro_slot]
        same_image = segment[:, None] == segment[None, :]
        factor = factor_all[micro_slot]
        branch_pick = jnp.where(active, 1 + section_kind, 0)
        produced = lax.switch(
            branch_pick, (spare_forward, attention_run, feedforward_run), hidden, factor, same_image
        )
        stash = lax.dynamic_update_index_in_dim(
            stash, jnp.where(active, hidden, stash[micro_slot]), micro_slot, 0
        )
        finished = jnp.where(
            active & (section_id == sections - 1),
            produced.astype(jnp.float32),
            block_all[micro_slot],
        )
        block_all = lax.dynamic_update_index_in_dim(block_all, finished, micro_slot, 0)
        if clock_tick + 1 < clocks:
            incoming = jax.tree.map(
                lambda part, own: part.astype(own.dtype),
                passed_along(shortened(produced), "section", 1),
                produced,
            )
    barrier_params = lax.optimization_barrier((local_vectors, local_attention, local_feedforward))
    back_weights = (
        lax.all_gather(barrier_params[0], "dp", axis=1, tiled=True),
        lax.all_gather(barrier_params[1], "dp", axis=0, tiled=True),
        lax.all_gather(barrier_params[2], "dp", axis=1, tiled=True),
    )

    def spare_backward(hidden, upstream, factor, same_image, totals):
        return (jnp.zeros((row_count, feature_count), jnp.float32), totals)

    def attention_back_run(hidden, upstream, factor, same_image, totals):
        hidden_grad, vector_piece, attention_piece = attention_backward(
            hidden, upstream, back_weights[0], back_weights[1], factor, same_image
        )
        return (hidden_grad, (totals[0] + vector_piece, totals[1] + attention_piece, totals[2]))

    def feedforward_back_run(hidden, upstream, factor, same_image, totals):
        hidden_grad, vector_piece, feedforward_piece = feedforward_backward(
            hidden, upstream, back_weights[0], back_weights[2], factor
        )
        return (hidden_grad, (totals[0] + vector_piece, totals[1], totals[2] + feedforward_piece))

    grad_totals = (
        jnp.zeros(back_weights[0].shape, jnp.float32),
        jnp.zeros(back_weights[1].shape, jnp.float32),
        jnp.zeros(back_weights[2].shape, jnp.float32),
    )
    input_all = jnp.zeros((micro_count, row_count, feature_count), jnp.float32)
    returning = jnp.zeros((row_count, feature_count), jnp.bfloat16)
    for clock_tick in range(clocks):
        position = clock_tick - (sections - 1 - section_id)
        active = (position >= 0) & (position < micro_count)
        micro_slot = jnp.clip(position, 0, micro_count - 1)
        upstream = jnp.where(
            section_id == sections - 1,
            output_grad[micro_slot].astype(jnp.float32),
            returning.astype(jnp.float32),
        )
        segment = segment_all[micro_slot]
        same_image = segment[:, None] == segment[None, :]
        factor = factor_all[micro_slot]
        branch_pick = jnp.where(active, 1 + section_kind, 0)
        hidden_grad, grad_totals = lax.switch(
            branch_pick,
            (spare_backward, attention_back_run, feedforward_back_run),
            stash[micro_slot],
            upstream,
            factor,
            same_image,
            grad_totals,
        )
        first_grad = jnp.where(active & (section_id == 0), hidden_grad, input_all[micro_slot])
        input_all = lax.dynamic_update_index_in_dim(input_all, first_grad, micro_slot, 0)
        if clock_tick + 1 < clocks:
            returning = passed_along(hidden_grad.astype(jnp.bfloat16), "section", -1)
    vector_total, attention_total, feedforward_total = grad_totals
    vector_sum, attention_sum, feedforward_sum = (
        lax.psum_scatter(vector_total, "dp", scatter_dimension=1, tiled=True),
        lax.psum_scatter(attention_total, "dp", scatter_dimension=0, tiled=True),
        lax.psum_scatter(feedforward_total, "dp", scatter_dimension=1, tiled=True),
    )
    vector_grad, attention_grad, feedforward_grad = lax.psum(
        (
            place_layer(vector_sum, layer_id, layer_total),
            place_layer(attention_sum, layer_id, layer_total),
            place_layer(feedforward_sum, layer_id, layer_total),
        ),
        "section",
    )
    block_sum, input_result = (
        lax.psum_scatter(
            block_all.astype(jnp.bfloat16), "section", scatter_dimension=2, tiled=True
        ).astype(jnp.float32),
        lax.psum_scatter(
            input_all.astype(jnp.bfloat16), "section", scatter_dimension=2, tiled=True
        ).astype(jnp.float32),
    )
    block_result = block_sum.astype(jnp.bfloat16)
    vector_mean, vector_square, vector_step = adam_update(
        vector_params, vector_first, vector_second, vector_grad, layer_rates, 0.0
    )
    attention_mean, attention_square, attention_step = adam_update(
        attention_weights,
        attention_first,
        attention_second,
        attention_grad,
        layer_rates,
        decay_rate,
    )
    feedforward_mean, feedforward_square, feedforward_step = adam_update(
        feedforward_weights,
        feedforward_first,
        feedforward_second,
        feedforward_grad,
        layer_rates,
        decay_rate,
    )
    return (
        block_result,
        input_result,
        vector_grad,
        attention_grad,
        feedforward_grad,
        vector_mean,
        attention_mean,
        feedforward_mean,
        vector_square,
        attention_square,
        feedforward_square,
        vector_step,
        attention_step,
        feedforward_step,
    )


def solution(mesh):
    in_specs = (
        P(None, "dp", None),
        P(),
        P(None, "dp", None),
        P(None, "dp", None, None),
        P(None, "dp", None),
        P(None, None, "dp"),
        P(None, "dp", None),
        P(None, None, "dp", None),
        P(None, None, "dp"),
        P(None, "dp", None),
        P(None, None, "dp", None),
        P(None, None, "dp"),
        P(None, "dp", None),
        P(None, None, "dp", None),
        P(),
    )
    out_specs = (
        P(None, "dp", "section"),
        P(None, "dp", "section"),
        P(None, None, "dp"),
        P(None, "dp", None),
        P(None, None, "dp", None),
        P(None, None, "dp"),
        P(None, "dp", None),
        P(None, None, "dp", None),
        P(None, None, "dp"),
        P(None, "dp", None),
        P(None, None, "dp", None),
        P(None, None, "dp"),
        P(None, "dp", None),
        P(None, None, "dp", None),
    )
    return jax.shard_map(shards, mesh=mesh, in_specs=in_specs, out_specs=out_specs, check_vma=False)
```

profile of v0, /device:TPU:0, one launch (start us, length us, event | category | flops | bytes accessed | tf_op | source)
XLA Modules:
  0.0 1640.9 jit_solution(6510318877925841902)
XLA Ops:
  20.0 17.6 %all-gather = bf16[1,12,768]{1,0,2:T(2,128)(2,1)S(1)} all-gather(bf16[1,12,96]{1,0,2:T(2,128)(2,1)S(1)} %copy.456), channel_id=2, replica_groups=mesh['section'=4,'dp'=8] {'dp'}, dimensions={2}, use_global_device_ids=true | all-gather | bytes 20736 | tf_op jit(solution)/shard_map/all_gather | solution.py:308
  49.8 17.9 %all-gather.13.cloned.1.call-done = bf16[1,768,3072]{2,1,0:T(8,128)(2,1)} async-done(((bf16[1,96,3072]{2,1,0:T(8,128)(2,1)}), bf16[1,768,3072]{2,1,0:T(8,128)(2,1)}) %all-gather.13.cloned.1.call-update) | async-done | bytes 4718608 | tf_op jit(solution)/shard_map/all_gather | solution.py:309
  67.7 91.8 %all-gather.15.cloned.1.call-done = bf16[1,2,768,3072]{3,2,1,0:T(8,128)(2,1)} async-done(((bf16[1,2,96,3072]{3,2,1,0:T(8,128)(2,1)}), bf16[1,2,768,3072]{3,2,1,0:T(8,128)(2,1)}) %all-gather.15.cloned.1.call-update) | async-done | bytes 9437200 | tf_op jit(solution)/shard_map/all_gather | solution.py:310
  159.6 47.1 %conditional.10 = (bf16[640,768]{1,0:T(8,128)(2,1)S(1)}, f32[640,768]{1,0:T(8,128)}) conditional(s32[]{:T(128)} %clamp.30, () %tuple.191, (f32[1,640]{1,0:T(1,128)S(1)}, f32[640,768]{1,0:T(8,128)S(1)}, bf16[12,768]{1,0:T(8,128)(2,1)S(1)}, bf16[768,3072]{1,0:T(8,128)(2,1)}, s32[2,640]{1,0:T(2,128)S(1)}, ...), branch_computations={%region_5.6_spmd, %region_6.11_spmd, %region_11.14_spmd} | conditional | flops 6058481664 | bytes 79419456 | solution.py:342
  210.7 18.9 %collective-permute-done = bf16[640,768]{1,0:T(8,128)(2,1)} collective-permute-done((bf16[640,768]{1,0:T(8,128)(2,1)S(1)}, bf16[640,768]{1,0:T(8,128)(2,1)}, u32[]{:S(2)}, u32[]{:S(2)}) %collective-permute-start) | collective-permute-done | bytes 983072 | tf_op jit(solution)/shard_map/ppermute | solution.py:37
  232.5 47.6 %conditional.11 = (bf16[640,768]{1,0:T(8,128)(2,1)S(1)}, f32[640,768]{1,0:T(8,128)}) conditional(s32[]{:T(128)} %clamp.31, () %tuple.194, (f32[1,640]{1,0:T(1,128)S(1)}, f32[640,768]{1,0:T(8,128)S(1)}, bf16[12,768]{1,0:T(8,128)(2,1)S(1)}, bf16[768,3072]{1,0:T(8,128)(2,1)}, s32[2,640]{1,0:T(2,128)S(1)}, ...), branch_computations={%region_14.15_spmd, %region_15.20_spmd, %region_20.23_spmd} | conditional | flops 6058481664 | bytes 79419456 | solution.py:342
  282.3 15.5 all-gather.3
  327.5 15.5 collective-permute-done.2
  385.3 23.3 %conditional.15 = (f32[640,768]{1,0:T(8,128)}, f32[12,768]{1,0:T(8,128)S(1)}, f32[768,3072]{1,0:T(8,128)}, f32[2,768,3072]{2,1,0:T(8,128)}) conditional(s32[]{:T(128)} %clamp.35, () %tuple.206, (f32[640,768]{1,0:T(8,128)S(1)}, bf16[12,768]{1,0:T(8,128)(2,1)S(1)}, bf16[768,3072]{1,0:T(8,128)(2,1)}, s32[2,640]{1,0:T(2,128)S(1)}, ...), branch_computations={%region_51.52_spmd, %region_52.64_spmd, %region_64.73_spmd} | conditional | flops 15158772736 | bytes 334967680 | solution.py:402
  412.6 60.7 %collective-permute-done.4 = bf16[640,768]{1,0:T(8,128)(2,1)S(1)} collective-permute-done((bf16[640,768]{1,0:T(8,128)(2,1)}, bf16[640,768]{1,0:T(8,128)(2,1)S(1)}, u32[]{:S(2)}, u32[]{:S(2)}) %collective-permute-start.4) | collective-permute-done | bytes 983072 | tf_op jit(solution)/shard_map/ppermute | solution.py:37
  489.7 22.9 %collective-permute-done.5 = bf16[640,768]{1,0:T(8,128)(2,1)S(1)} collective-permute-done((bf16[640,768]{1,0:T(8,128)(2,1)}, bf16[640,768]{1,0:T(8,128)(2,1)S(1)}, u32[]{:S(2)}, u32[]{:S(2)}) %collective-permute-start.5) | collective-permute-done | bytes 983072 | tf_op jit(solution)/shard_map/ppermute | solution.py:37
  529.0 228.4 %collective-permute-done.6 = bf16[640,768]{1,0:T(8,128)(2,1)S(1)} collective-permute-done((bf16[640,768]{1,0:T(8,128)(2,1)}, bf16[640,768]{1,0:T(8,128)(2,1)S(1)}, u32[]{:S(2)}, u32[]{:S(2)}) %collective-permute-start.6) | collective-permute-done | bytes 983072 | tf_op jit(solution)/shard_map/ppermute | solution.py:37
  760.0 120.4 %conditional.18 = (f32[640,768]{1,0:T(8,128)}, f32[12,768]{1,0:T(8,128)S(1)}, f32[768,3072]{1,0:T(8,128)}, f32[2,768,3072]{2,1,0:T(8,128)}) conditional(s32[]{:T(128)} %clamp.38, (f32[12,768]{1,0:T(8,128)S(1)}, f32[768,3072]{1,0:T(8,128)}, f32[2,768,3072]{2,1,0:T(8,128)}) %tuple.216, (f32[640,768]{1,0:T(8,128)S(1)}, ...), branch_computations={%region_117.118_spmd, %region_118.130_spmd, %region_130.139_spmd} | conditional | flops 15163500544 | bytes 325641088 | solution.py:402
  803.3 16.7 %multiply_reduce_fusion.37 = (f32[12,640]{1,0:T(8,128)S(1)}, f32[12,640,640]{1,2,0:T(8,128)}) fusion(f32[12,640,640]{1,2,0:T(8,128)} %get-tuple-element.1341, f32[12,640]{1,0:T(8,128)S(1)} %get-tuple-element.1340, bf16[640,12,64]{0,2,1:T(8,128)(2,1)} %bitcast.646, bf16[640,12,64]{0,2,1:T(8,128)(2,1)} %bitcast.633), kind=kOutput, calls=%fused_computation.553 | convolution fusion | flops 643883520 | bytes 41349120 | tf_op jit(solution)/shard_map/cond/branch_1_fun/qhd,khd->hqk/dot_general | solution.py:155
  819.9 13.4 multiply_convert_fusion.26
  884.5 20.0 %collective-permute-done.7 = bf16[640,768]{1,0:T(8,128)(2,1)S(1)} collective-permute-done((bf16[640,768]{1,0:T(8,128)(2,1)}, bf16[640,768]{1,0:T(8,128)(2,1)S(1)}, u32[]{:S(2)}, u32[]{:S(2)}) %collective-permute-start.7) | collective-permute-done | bytes 983072 | tf_op jit(solution)/shard_map/ppermute | solution.py:37
  907.2 130.4 %conditional.19 = (f32[640,768]{1,0:T(8,128)}, f32[12,768]{1,0:T(8,128)S(1)}, f32[768,3072]{1,0:T(8,128)}, f32[2,768,3072]{2,1,0:T(8,128)}) conditional(s32[]{:T(128)} %clamp.39, (f32[12,768]{1,0:T(8,128)S(1)}, f32[768,3072]{1,0:T(8,128)}, f32[2,768,3072]{2,1,0:T(8,128)}) %tuple.219, (f32[640,768]{1,0:T(8,128)S(1)}, ...), branch_computations={%region_139.140_spmd, %region_140.152_spmd, %region_152.161_spmd} | conditional | flops 15163500544 | bytes 325641088 | solution.py:402
  961.1 16.7 %multiply_reduce_fusion.46 = (f32[12,640]{1,0:T(8,128)S(1)}, f32[12,640,640]{1,2,0:T(8,128)}) fusion(f32[12,640,640]{1,2,0:T(8,128)} %get-tuple-element.1356, f32[12,640]{1,0:T(8,128)S(1)} %get-tuple-element.1355, bf16[640,12,64]{0,2,1:T(8,128)(2,1)} %bitcast.648, bf16[640,12,64]{0,2,1:T(8,128)(2,1)} %bitcast.635), kind=kOutput, calls=%fused_computation.644 | convolution fusion | flops 643883520 | bytes 41349120 | tf_op jit(solution)/shard_map/cond/branch_1_fun/qhd,khd->hqk/dot_general | solution.py:155
  1077.2 56.8 %reduce-scatter.6.cloned.1.call-done = f32[96,3072]{1,0:T(8,128)} async-done(((f32[768,3072]{1,0:T(8,128)}), f32[96,3072]{1,0:T(8,128)}) %reduce-scatter.6.cloned.1.call-update) | async-done | bytes 1179664 | tf_op jit(solution)/shard_map/reduce_scatter | solution.py:418
  1136.8 185.8 %reduce-scatter.8.cloned.1.call-done = f32[2,96,3072]{2,1,0:T(8,128)} async-done(((f32[2,768,3072]{2,1,0:T(8,128)}), f32[2,96,3072]{2,1,0:T(8,128)}) %reduce-scatter.8.cloned.1.call-update) | async-done | bytes 2359312 | tf_op jit(solution)/shard_map/reduce_scatter | solution.py:419
  1328.8 25.7 %reduce-scatter.10.cloned.1.call-done = f32[96,12]{1,0:T(8,128)} async-done(((f32[768,12]{1,0:T(8,128)}), f32[96,12]{1,0:T(8,128)}) %reduce-scatter.10.cloned.1.call-update) | async-done | bytes 4624
  1355.5 16.2 psum.21
  1372.3 84.9 %all-reduce.9.cloned.1.call-done = (bf16[2,640,768]{1,0,2:T(2,128)(2,1)}, bf16[2,640,768]{1,0,2:T(2,128)(2,1)}) async-done(((bf16[2,640,768]{1,0,2:T(2,128)(2,1)}, bf16[2,640,768]{1,0,2:T(2,128)(2,1)}), (bf16[2,640,768]{1,0,2:T(2,128)(2,1)}, bf16[2,640,768]{1,0,2:T(2,128)(2,1)})) %all-reduce.9.cloned.1.call-update) | async-done | bytes 3932176
  1461.9 151.4 %all-reduce.7.cloned.1.call-done = (f32[2,96,3072]{2,1,0:T(8,128)}, f32[2,2,96,3072]{3,2,1,0:T(8,128)}) async-done(((f32[2,96,3072]{2,1,0:T(8,128)}, f32[2,2,96,3072]{3,2,1,0:T(8,128)}), (f32[2,96,3072]{2,1,0:T(8,128)}, f32[2,2,96,3072]{3,2,1,0:T(8,128)})) %all-reduce.7.cloned.1.call-update) | async-done | bytes 7077904 | tf_op jit(solution)/shard_map/psum | solution.py:421
  (391 shorter events, 507.0 us)
Async XLA Ops:
  7.2 60.5 %all-gather.13.cloned.1.call-start = ((), (), s32[]{:S(2)}) async-start(), calls=%async_computation.7 | async-start | bytes 5308416 | tf_op jit(solution)/shard_map/all_gather | solution.py:309
  9.5 150.0 %all-gather.15.cloned.1.call-start = ((), (), s32[]{:S(2)}) async-start(), calls=%async_computation.8 | async-start | bytes 10616832 | tf_op jit(solution)/shard_map/all_gather | solution.py:310
  12.5 372.8 %all-gather.9.cloned.1.call-start = ((), (), s32[]{:S(2)}) async-start(), calls=%async_computation.3 | async-start | bytes 5308416 | tf_op jit(solution)/shard_map/all_gather | solution.py:363
  17.6 367.6 %all-gather.11.cloned.1.call-start = ((), (), s32[]{:S(2)}) async-start(), calls=%async_computation.4 | async-start | bytes 10616832 | tf_op jit(solution)/shard_map/all_gather | solution.py:364
  18.2 1115.8 %reduce-scatter.6.cloned.1.call-start = ((), (), s32[]{:S(2)}) async-start(), calls=%async_computation.5 | async-start | bytes 10616832 | tf_op jit(solution)/shard_map/reduce_scatter | solution.py:418
  37.9 306.7 %copy-start.70 = (bf16[1,12,768]{2,1,0:T(8,128)(2,1)}, bf16[1,12,768]{2,1,0:T(8,128)(2,1)S(1)}, u32[]{:S(2)}) copy-start(bf16[1,12,768]{2,1,0:T(8,128)(2,1)S(1)} %copy.457) | copy-start | bytes 55300
  206.6 22.9 %collective-permute-start = (bf16[640,768]{1,0:T(8,128)(2,1)S(1)}, bf16[640,768]{1,0:T(8,128)(2,1)}, u32[]{:S(2)}, u32[]{:S(2)}) collective-permute-start(bf16[640,768]{1,0:T(8,128)(2,1)S(1)} %get-tuple-element.895), channel_id=1, source_target_pairs={{0,8},{8,16},{16,24},{1,9},{9,17},{17,25},{2,10},{10,18},{18,26},{... | collective-permute-start | bytes 2949128 | tf_op jit(solution)/shard_map/ppermute | solution.py:37
  280.1 23.1 %collective-permute-start.1 = (bf16[640,768]{1,0:T(8,128)(2,1)S(1)}, bf16[640,768]{1,0:T(8,128)(2,1)}, u32[]{:S(2)}, u32[]{:S(2)}) collective-permute-start(bf16[640,768]{1,0:T(8,128)(2,1)S(1)} %get-tuple-element.897), channel_id=1, source_target_pairs={{0,8},{8,16},{16,24},{1,9},{9,17},{17,25},{2,10},{10,18},{18,26},{... | collective-permute-start | bytes 2949128 | tf_op jit(solution)/shard_map/ppermute | solution.py:37
  316.1 26.9 %collective-permute-start.2 = (bf16[640,768]{1,0:T(8,128)(2,1)S(1)}, bf16[640,768]{1,0:T(8,128)(2,1)S(1)}, u32[]{:S(2)}, u32[]{:S(2)}) collective-permute-start(bf16[640,768]{1,0:T(8,128)(2,1)S(1)} %get-tuple-element.899), channel_id=1, source_target_pairs={{0,8},{8,16},{16,24},{1,9},{9,17},{17,25},{2,10},{10,18},{18,26},{... | collective-permute-start | bytes 2949128 | tf_op jit(solution)/shard_map/ppermute | solution.py:37
  350.1 25.4 %collective-permute-start.3 = (bf16[640,768]{1,0:T(8,128)(2,1)S(1)}, bf16[640,768]{1,0:T(8,128)(2,1)S(1)}, u32[]{:S(2)}, u32[]{:S(2)}) collective-permute-start(bf16[640,768]{1,0:T(8,128)(2,1)S(1)} %get-tuple-element.901), channel_id=1, source_target_pairs={{0,8},{8,16},{16,24},{1,9},{9,17},{17,25},{2,10},{10,18},{18,26},{... | collective-permute-start | bytes 2949128 | tf_op jit(solution)/shard_map/ppermute | solution.py:37
  408.5 67.5 %copy-start.5 = (f32[640,768]{1,0:T(8,128)S(1)}, f32[640,768]{1,0:T(8,128)}, u32[]{:S(2)}) copy-start(f32[640,768]{1,0:T(8,128)} %get-tuple-element.1368) | copy-start | bytes 5898244
  408.6 67.4 %copy-start.106 = (f32[1,640]{1,0:T(1,128)S(1)}, f32[1,640]{1,0:T(1,128)}, u32[]{:S(2)}) copy-start(f32[1,640]{1,0:T(1,128)} %get-tuple-element.1375) | copy-start | bytes 7684
  411.3 62.0 %collective-permute-start.4 = (bf16[640,768]{1,0:T(8,128)(2,1)}, bf16[640,768]{1,0:T(8,128)(2,1)S(1)}, u32[]{:S(2)}, u32[]{:S(2)}) collective-permute-start(bf16[640,768]{1,0:T(8,128)(2,1)} %convert_element_type.1061), channel_id=1, source_target_pairs={{8,0},{16,8},{24,16},{9,1},{17,9},{25,17},{10,2},{18,10},{26,18},{... | collective-permute-start | bytes 2949128 | tf_op jit(solution)/shard_map/ppermute | solution.py:37
  488.4 24.2 %collective-permute-start.5 = (bf16[640,768]{1,0:T(8,128)(2,1)}, bf16[640,768]{1,0:T(8,128)(2,1)S(1)}, u32[]{:S(2)}, u32[]{:S(2)}) collective-permute-start(bf16[640,768]{1,0:T(8,128)(2,1)} %convert_element_type.1065), channel_id=1, source_target_pairs={{8,0},{16,8},{24,16},{9,1},{17,9},{25,17},{10,2},{18,10},{26,18},{... | collective-permute-start | bytes 2949128 | tf_op jit(solution)/shard_map/ppermute | solution.py:37
  525.0 235.1 %copy-start.3 = (f32[640,768]{1,0:T(8,128)S(1)}, f32[640,768]{1,0:T(8,128)}, u32[]{:S(2)}) copy-start(f32[640,768]{1,0:T(8,128)} %get-tuple-element.1366) | copy-start | bytes 5898244
  525.0 235.1 %copy-start.104 = (f32[1,640]{1,0:T(1,128)S(1)}, f32[1,640]{1,0:T(1,128)}, u32[]{:S(2)}) copy-start(f32[1,640]{1,0:T(1,128)} %get-tuple-element.1373) | copy-start | bytes 7684
  527.7 229.7 %collective-permute-start.6 = (bf16[640,768]{1,0:T(8,128)(2,1)}, bf16[640,768]{1,0:T(8,128)(2,1)S(1)}, u32[]{:S(2)}, u32[]{:S(2)}) collective-permute-start(bf16[640,768]{1,0:T(8,128)(2,1)} %convert_element_type.1069), channel_id=1, source_target_pairs={{8,0},{16,8},{24,16},{9,1},{17,9},{25,17},{10,2},{18,10},{26,18},{... | collective-permute-start | bytes 2949128 | tf_op jit(solution)/shard_map/ppermute | solution.py:37
  883.2 21.3 %collective-permute-start.7 = (bf16[640,768]{1,0:T(8,128)(2,1)}, bf16[640,768]{1,0:T(8,128)(2,1)S(1)}, u32[]{:S(2)}, u32[]{:S(2)}) collective-permute-start(bf16[640,768]{1,0:T(8,128)(2,1)} %convert_element_type.1073), channel_id=1, source_target_pairs={{8,0},{16,8},{24,16},{9,1},{17,9},{25,17},{10,2},{18,10},{26,18},{... | collective-permute-start | bytes 2949128 | tf_op jit(solution)/shard_map/ppermute | solution.py:37
  1037.6 285.0 %reduce-scatter.8.cloned.1.call-start = ((), (), s32[]{:S(2)}) async-start(), calls=%async_computation.6 | async-start | bytes 21233664 | tf_op jit(solution)/shard_map/reduce_scatter | solution.py:419
  1038.2 316.3 %reduce-scatter.10.cloned.1.call-start = ((), (), s32[]{:S(2)}) async-start(), calls=%async_computation.9 | async-start | bytes 442368
  1067.1 390.2 %all-reduce.9.cloned.1.call-start = ((), (), s32[]{:S(2)}) async-start(), calls=%async_computation.11 | async-start | bytes 7864320
  1077.2 536.1 %all-reduce.7.cloned.1.call-start = ((), (), s32[]{:S(2)}) async-start(), calls=%async_computation.10 | async-start | bytes 14155776 | tf_op jit(solution)/shard_map/psum | solution.py:421
  1371.7 249.8 %copy-start.99 = (f32[2,12,96]{2,0,1:T(2,128)}, f32[2,12,96]{2,0,1:T(2,128)S(1)}, u32[]{:S(2)}) copy-start(f32[2,12,96]{2,0,1:T(2,128)S(1)} %psum.21) | copy-start | bytes 27652
  1458.6 162.9 %slice-start = ((s8[4718592]{0:T(1024)(128)(4,1)}), s8[524288]{0:T(1024)(128)(4,1)S(1)}, s32[]{:S(2)}) async-start(s8[4718592]{0:T(1024)(128)(4,1)} %bitcast.545), calls=%async_computation.12 | async-start | bytes 1048576
  (58 other events, 648.8 us)
Sparse Core Ops, SparseCore 0:
  10.3 57.4 all-gather.12
  69.9 89.6 all-gather.14
  161.2 50.1 all-gather.8
  212.9 89.7 all-gather.10
  1037.7 96.2 reduce-scatter.5
  1136.2 186.3 reduce-scatter.7
  1325.4 29.0 reduce-scatter.9
  1358.5 98.6 all-reduce.8
  1461.5 151.7 all-reduce.6
where the time goes:
time: 1650 us; the launch traced here: 1640 us
  waiting for transfers between devices  991 us (60%)
  matrix products  203 us (12%)
  local copies, waits for them, and re-layouts  139 us (8%)
  other arithmetic  134 us (8%)
  loops' own time  86.7 us (5%)
  blocking collectives  49.3 us (3%)
  starting transfers between devices  22.8 us (1%)
    ppermute x8, waiting for transfers between devices, passed_along(): lax.ppermute(value, axis, [(source, source + steps) for source in range(i...  375 us
    reduce_scatter x1, waiting for transfers between devices, shards(): lax.psum_scatter(feedforward_total, 'dp', scatter_dimension=1, tiled=True)  186 us
    psum x1, waiting for transfers between devices, shards(): lax.psum((place_layer(vector_sum, layer_id, layer_total), place_layer(att...  151 us
    unnamed x11, waiting for transfers between devices  112 us
    all_gather x1, waiting for transfers between devices, shards(): lax.all_gather(local_feedforward, 'dp', axis=1, tiled=True)  91.8 us
    reduce_scatter x1, waiting for transfers between devices, shards(): lax.psum_scatter(attention_total, 'dp', scatter_dimension=0, tiled=True)  56.8 us
    another operation x5, loops' own time, shards(): lax.switch(branch_pick, (spare_backward, attention_back_run, feedforward_...  48.5 us
    sub x4, matrix products, attention_parts(): exp_scores = jnp.exp(scores - row_peak)  48.1 us
  transfers between devices with their start and end apart: 17, of which 14 were waited for; matrix products, arithmetic and copies ran while one was open for 11% of the time, Pallas kernels for 0%

commit v1 on v0

v1 whole, which is shorter than its diff:
```python
import functools

import jax
import jax.numpy as jnp
from jax import lax
from jax.experimental import pallas as pl
from jax.experimental.pallas import tpu as pltpu
from jax.sharding import PartitionSpec as P

H = 12
HD = 64
GRID_S = 10
GRID_M = 14
GRID_L = 24

beta_one = 0.9
beta_two = 0.999
bias_one = 1.0 - 0.9**10
bias_two = 1.0 - 0.999**10
adam_eps = 1e-08
decay_rate = 0.05
drop_rate = 0.1
norm_eps = 1e-06
masked_score = -1e30
root_half = 0.7071067811865476
normal_peak = 0.3989422804014327
BF = jnp.bfloat16
F32 = jnp.float32


def image_layout(image_ids, row_count):
    small_len = GRID_S * GRID_S + 2
    middle_len = GRID_M * GRID_M + 2
    large_len = GRID_L * GRID_L + 2
    slots = image_ids.shape[0]
    lengths = jnp.where(
        image_ids == 0,
        small_len,
        jnp.where(image_ids == 1, middle_len, jnp.where(image_ids == 2, large_len, 0)),
    ).astype(jnp.int32)
    slot = jnp.arange(slots, dtype=jnp.int32)
    slot_ends = jnp.sum(jnp.where(slot[None, :] <= slot[:, None], lengths[None, :], 0), axis=1)
    slot_starts = slot_ends - lengths
    row_index = jnp.arange(row_count, dtype=jnp.int32)
    segment = jnp.sum((row_index[:, None] >= slot_ends[None, :]).astype(jnp.int32), axis=1)
    member = segment[:, None] == slot[None, :]
    first_row = jnp.sum(jnp.where(member, slot_starts[None, :], 0), axis=1)
    kind_row = jnp.sum(jnp.where(member, image_ids[None, :], 0), axis=1)
    table_start = jnp.where(
        kind_row == 0, 0, jnp.where(kind_row == 1, small_len, small_len + middle_len)
    ).astype(jnp.int32)
    in_image = segment < slots
    table_row = jnp.where(in_image, table_start + row_index - first_row, 0)
    return (segment, member, in_image, table_row)


def normalize(hidden, gain, shift):
    center = hidden - jnp.mean(hidden, axis=-1, keepdims=True)
    inverse = lax.rsqrt(jnp.mean(center * center, axis=-1, keepdims=True) + norm_eps)
    scaled = center * inverse
    return (scaled * gain + shift, scaled, inverse)


def normalize_back(normed_grad, scaled, inverse, gain):
    scaled_grad = normed_grad * gain
    centered = scaled_grad - jnp.mean(scaled_grad, axis=-1, keepdims=True)
    return inverse * (centered - scaled * jnp.mean(scaled_grad * scaled, axis=-1, keepdims=True))


def nn(a, b):
    return jnp.dot(a, b, preferred_element_type=F32)


def nt(a, b):
    return lax.dot_general(a, b, (((1,), (1,)), ((), ())), preferred_element_type=F32)


def tn(a, b):
    return lax.dot_general(a, b, (((0,), (0,)), ((), ())), preferred_element_type=F32)


def split3(value):
    high = value.astype(BF)
    rest = value - high.astype(F32)
    middle = rest.astype(BF)
    return high, middle, (rest - middle.astype(F32)).astype(BF)


def attention_kernel(q_ref, k_ref, v_ref, code_q_ref, code_k_ref, o_ref, lse_ref):
    low = lax.broadcasted_iota(jnp.int32, q_ref.shape, 1) < HD
    outs = []
    for half in range(2):
        own = low if half == 0 else jnp.logical_not(low)
        q = jnp.where(own, q_ref[...] * jnp.asarray(HD ** (-0.5), BF), code_q_ref[...])
        k = jnp.where(own, k_ref[...], code_k_ref[...])
        scores = nt(q, k)
        peak = jnp.max(scores, axis=-1, keepdims=True)
        e = jnp.exp(scores - peak)
        total = jnp.sum(e, axis=-1, keepdims=True)
        p = (e * (1.0 / total)).astype(BF)
        outs.append(nn(p, v_ref[...]))
        lse_ref[:, half : half + 1] = peak + jnp.log(total)
    o_ref[...] = jnp.where(low, outs[0], outs[1]).astype(BF)


def attention_back_kernel(
    q_ref, k_ref, v_ref, do_ref, lse_ref, code_q_ref, code_k_ref, dq_ref, dk_ref, dv_ref
):
    lane = lax.broadcasted_iota(jnp.int32, q_ref.shape, 1)
    low = lane < HD
    scale = HD ** (-0.5)
    dqs, dks, dvs = [], [], []
    for half in range(2):
        own = low if half == 0 else jnp.logical_not(low)
        spare = 32 + (HD if half == 0 else 0)
        q_scaled = q_ref[...] * jnp.asarray(scale, BF)
        q = jnp.where(own, q_scaled, code_q_ref[...])
        k = jnp.where(own, k_ref[...], code_k_ref[...])
        v = jnp.where(own, v_ref[...], jnp.zeros_like(v_ref[...]))
        for at, part in enumerate(split3(-lse_ref[:, half : half + 1])):
            here = lane == spare + at
            q = jnp.where(here, part, q)
            k = jnp.where(here, jnp.ones_like(k), k)
        p = jnp.exp(nt(k, q))
        dp = nt(v, do_ref[...])
        row = jnp.sum(p * dp, axis=0, keepdims=True)
        ds = (p * (dp - row)).astype(BF)
        dvs.append(nn(p.astype(BF), do_ref[...]))
        dks.append(nn(ds, q_scaled))
        dqs.append(tn(ds, k_ref[...]) * scale)
    dq_ref[...] = jnp.where(low, dqs[0], dqs[1]).astype(BF)
    dk_ref[...] = jnp.where(low, dks[0], dks[1]).astype(BF)
    dv_ref[...] = jnp.where(low, dvs[0], dvs[1]).astype(BF)


def attention(q, k, v, code_q, code_k):
    rows, width = q.shape
    pair = pl.BlockSpec((rows, 2 * HD), lambda i: (0, i))
    whole = pl.BlockSpec((rows, 2 * HD), lambda i: (0, 0))
    return pl.pallas_call(
        attention_kernel,
        grid=(width // (2 * HD),),
        in_specs=[pair, pair, pair, whole, whole],
        out_specs=[pair, pl.BlockSpec((None, rows, 2), lambda i: (i, 0, 0))],
        out_shape=[
            jax.ShapeDtypeStruct((rows, width), BF),
            jax.ShapeDtypeStruct((width // (2 * HD), rows, 2), F32),
        ],
        compiler_params=pltpu.CompilerParams(vmem_limit_bytes=48 * 2**20),
        name="attention",
    )(q, k, v, code_q, code_k)


def attention_back(q, k, v, do, lse, code_q, code_k):
    rows, width = q.shape
    pair = pl.BlockSpec((rows, 2 * HD), lambda i: (0, i))
    whole = pl.BlockSpec((rows, 2 * HD), lambda i: (0, 0))
    return pl.pallas_call(
        attention_back_kernel,
        grid=(width // (2 * HD),),
        in_specs=[pair] * 4
        + [pl.BlockSpec((None, rows, 2), lambda i: (i, 0, 0)), whole, whole],
        out_specs=[pair] * 3,
        out_shape=[jax.ShapeDtypeStruct((rows, width), BF)] * 3,
        compiler_params=pltpu.CompilerParams(vmem_limit_bytes=48 * 2**20),
        name="attention_back",
    )(q, k, v, do, lse, code_q, code_k)


def assemble_kernel(count, at_ref, *refs):
    sources, out_ref, sems = refs[:12], refs[12], refs[13]
    s, z, c = at_ref[0], at_ref[1], at_ref[2]
    share, width = sources[0].shape[2], sources[0].shape[3]
    half = width // 2
    for mat in range(count):

        def place(source, q, chip, core, left=0, size=width, mat=mat):
            row = pl.multiple_of((chip * 2 + core) * share, share)
            target = out_ref.at[mat, q, pl.ds(row, share), pl.ds(left, size)]
            pltpu.make_async_copy(source, target, sems.at[mat]).start()

        for turn in range(2):
            own, far, x_far, y_far, d_left, d_right = sources[turn::2]
            core = c if turn == 0 else 1 - c
            for q in range(4):
                place(own.at[mat, q], q, z, core)
            for k in range(3):
                chip = lax.rem(z + 3 - k, 4)
                place(far.at[k, mat], s, chip, core)
                place(x_far.at[k, mat], s ^ 1, chip, core)
                place(y_far.at[k, mat], s ^ 2, chip, core)
                place(d_left.at[k, mat], s ^ 3, chip, core, 0, half)
                place(d_right.at[k, mat], s ^ 3, chip, core, half, half)
    for mat in range(count):
        pltpu.make_async_copy(out_ref.at[mat], out_ref.at[mat], sems.at[mat]).wait()


def assemble(at, sources):
    count, _, share, width = sources[0].shape
    return pl.pallas_call(
        functools.partial(assemble_kernel, count),
        in_specs=[pl.BlockSpec(memory_space=pltpu.SMEM)] + [pl.BlockSpec(memory_space=pl.ANY)] * 12,
        out_specs=pl.BlockSpec(memory_space=pl.ANY),
        out_shape=jax.ShapeDtypeStruct((count, 4, 8 * share, width), BF),
        scratch_shapes=[pltpu.SemaphoreType.DMA((count,))],
        compiler_params=pltpu.CompilerParams(vmem_limit_bytes=2**20),
        name="assemble",
    )(at, *sources)


def adam_update(weight, first_moment, second_moment, gradient, layer_rates, decay_on):
    layer_rate = layer_rates.reshape((-1,) + (1,) * (weight.ndim - 1))
    mean_next = beta_one * first_moment + (1.0 - beta_one) * gradient
    square_next = beta_two * second_moment + (1.0 - beta_two) * gradient * gradient
    step_next = layer_rate * (
        mean_next / bias_one / (jnp.sqrt(square_next / bias_two) + adam_eps) + decay_on * weight
    )
    return (mean_next, square_next, step_next)


def shards(
    patches,
    positions,
    image_sizes,
    keep_masks,
    output_grad,
    vector_params,
    attention_weights,
    feedforward_weights,
    vector_first,
    attention_first,
    feedforward_first,
    vector_second,
    attention_second,
    feedforward_second,
    layer_rates,
):
    both = ("section", "dp")
    micro_count, row_count, width = patches.shape
    layers = vector_params.shape[0]
    share = attention_weights.shape[1]
    half = width // 2
    s = lax.axis_index("section")
    s_low, s_high = s % 2, s // 2
    unit = s_low ^ s_high
    across = [(i, i ^ 1) for i in range(4)]
    along = [(i, i ^ 2) for i in range(4)]

    def quarter(array):
        return lax.dynamic_slice_in_dim(array, s * width, width, axis=array.ndim - 1)

    shards_dp = lax.axis_size("dp")
    d = lax.axis_index("dp")
    packed = (
        (attention_weights[0],),
        (feedforward_weights[0, 0], feedforward_weights[0, 1]),
        (attention_weights[1],),
        (feedforward_weights[1, 0], feedforward_weights[1, 1]),
    )
    if shards_dp == 8:
        around = [[(i, (i + 2 * k) % 8) for i in range(8)] for k in (1, 2, 3)]
        swap = [(i, i ^ 1) for i in range(8)]
        at = jnp.stack([s, d // 2, d % 2]).astype(jnp.int32)
        flat = vector_params.astype(BF).reshape(-1, share * 8)
        flat = jnp.pad(flat, ((0, 16 - flat.shape[0]), (0, 0)))
        mats, vector_pieces = [], None
        for group, members in enumerate(packed):
            count = len(members)
            own = jnp.stack([quarter(w).astype(BF) for w in members])
            blocks = jnp.stack(
                [w.astype(BF).reshape(share, 4, width).transpose(1, 0, 2) for w in members]
            )
            sent = own.reshape(-1, width)
            if group == 0:
                sent = jnp.concatenate([sent, flat])
            far = [lax.ppermute(sent, "dp", route) for route in around]
            if group == 0:
                vector_pieces = jnp.stack([flat] + [f[count * share :] for f in far])
                far = [f[: count * share] for f in far]
            far = jnp.stack(far).reshape(3, count, share, width)
            x_far = lax.ppermute(far, "section", across)
            y_far = lax.ppermute(far, "section", along)
            d_left = lax.ppermute(y_far[..., :half], "section", across)
            d_right = lax.ppermute(x_far[..., half:], "section", along)
            sources = []
            for piece in (blocks, far, x_far, y_far, d_left, d_right):
                sources += [piece, lax.ppermute(piece, "dp", swap)]
            mats.append(assemble(at, sources))
        both_cores = jnp.stack([vector_pieces, lax.ppermute(vector_pieces, "dp", swap)])
        chips = (d // 2 - jnp.arange(4)) % 4
        order = jnp.where(jnp.arange(4)[:, None] == chips[None, :], 1.0, 0.0).astype(BF)
        both_cores = jnp.einsum("zk,kcrw->zcrw", order, both_cores.transpose(1, 0, 2, 3))
        ordered = jnp.where(d % 2 == 0, both_cores, both_cores[:, ::-1])
        ordered = ordered.reshape(8, -1)[:, : layers * 12 * share].reshape(8, layers, 12, share)
        vectors = ordered.transpose(1, 2, 0, 3).reshape(layers, 12, width).astype(F32)
        weights = [(mats[2 * l][0], mats[2 * l + 1][0], mats[2 * l + 1][1]) for l in range(layers)]
    else:

        def gathered(piece):
            piece = lax.all_gather(quarter(piece).astype(BF), both, axis=0, tiled=True)
            return piece.reshape(4, width, width)

        vectors = lax.all_gather(vector_params.astype(BF), "dp", axis=2, tiled=True).astype(F32)
        mats = [[gathered(w) for w in members] for members in packed]
        weights = [(mats[2 * l][0], mats[2 * l + 1][0], mats[2 * l + 1][1]) for l in range(layers)]

    image_ids = lax.dynamic_index_in_dim(image_sizes[:, 0], unit, 0, keepdims=False)
    keep = lax.dynamic_index_in_dim(keep_masks[:, 0], unit, 0, keepdims=False)
    segment, member, inside, table_row = image_layout(image_ids, row_count)
    kept = jnp.sum(jnp.where(member[:, :, None], keep[None], 0), axis=1).astype(F32)
    factors = jnp.where(inside[:, None], kept / (1.0 - drop_rate), 1.0)
    patch_rows = lax.dynamic_index_in_dim(patches, unit, 0, keepdims=False).astype(F32)
    position_rows = jnp.take(positions, table_row, axis=0).astype(F32)
    hidden = patch_rows + jnp.where(inside[:, None], position_rows, 0.0)
    lane = jnp.arange(2 * HD, dtype=jnp.int32) % HD
    coded = lane[None, :] == segment[:, None]
    code_q = coded.astype(BF)
    code_k = jnp.where(coded | (lane[None, :] > image_sizes.shape[2]), 0.0, masked_score).astype(BF)

    saved = []
    for layer in range(layers):
        wa, w1, w2 = weights[layer]
        vec = [vectors[layer, i : i + 1] for i in range(12)]
        fa = factors[:, 2 * layer : 2 * layer + 1]
        ff = factors[:, 2 * layer + 1 : 2 * layer + 2]
        a, scaled, inverse = normalize(hidden, vec[0], vec[1])
        a = a.astype(BF)
        q = (nn(a, wa[0]) + vec[2]).astype(BF)
        k = nn(a, wa[1]).astype(BF)
        v = (nn(a, wa[2]) + vec[3]).astype(BF)
        o, lse = attention(q, k, v, code_q, code_k)
        mid = (hidden + fa * (nn(o, wa[3]) + vec[4])).astype(BF).astype(F32)
        a2, scaled2, inverse2 = normalize(mid, vec[5], vec[6])
        a2 = a2.astype(BF)
        gbs, slopes = [], []
        branch = vec[7]
        for part in range(4):
            u = nn(a2, w1[part]) + vec[8 + part]
            cdf = 0.5 * (1.0 + lax.erf(u * root_half))
            gb = (u * cdf).astype(BF)
            slopes.append(cdf + u * jnp.exp(-0.5 * u * u) * normal_peak)
            gbs.append(gb)
            branch = branch + nt(gb, w2[part])
        saved.append((hidden, a, q, k, v, o, lse, mid, a2, gbs, slopes))
        hidden = (mid + ff * branch).astype(BF).astype(F32)

    def pick(index, options):
        value = options[0]
        for at in range(1, len(options)):
            value = jnp.where(index == at, options[at], value)
        return value

    def reduced(pairs, rows):
        count = len(pairs)
        summed = []
        extra = jnp.pad(jnp.concatenate(rows), ((0, 128 - len(rows)), (0, 0))).T.astype(BF)
        for xy, (side, route) in enumerate(((s_low, across), (s_high, along))):
            parts = [pair[xy].astype(BF) for pair in pairs]
            mine = [lax.dynamic_slice_in_dim(part, side * half, half, 1) for part in parts]
            other = [lax.dynamic_slice_in_dim(part, (1 - side) * half, half, 1) for part in parts]
            if xy == 0:
                mine.append(extra)
                other.append(extra)
            mine = jnp.concatenate(mine, axis=1)
            other = lax.ppermute(jnp.concatenate(other, axis=1), "section", route)
            summed.append((mine.astype(F32) + other.astype(F32)).astype(BF))
        stacked = jnp.concatenate(summed, axis=1)
        scattered = lax.psum_scatter(stacked, "dp", scatter_dimension=0, tiled=True)
        cut = count * half
        vector = scattered[:, cut : cut + len(rows)].astype(F32).T
        everyone = jnp.concatenate([scattered[:, :cut], scattered[:, cut + 128 :]], axis=1)
        everyone = lax.all_gather(everyone, "section", axis=0, tiled=False)
        everyone = everyone.reshape(4, share, 2, count, half)
        order = ((0, 0), (1, 0), (0, 1), (2, 1), (2, 0), (3, 0), (1, 1), (3, 1))
        return vector, [
            jnp.concatenate([everyone[dev, :, xy, mat] for dev, xy in order], axis=1).astype(F32)
            for mat in range(count)
        ]

    up = lax.dynamic_index_in_dim(output_grad, unit, 0, keepdims=False).astype(F32)
    vector_grads = [None] * layers
    attention_grads = [None] * layers
    feed_grads = [None] * layers
    for layer in reversed(range(layers)):
        wa, w1, w2 = weights[layer]
        vec = [vectors[layer, i : i + 1] for i in range(12)]
        fa = factors[:, 2 * layer : 2 * layer + 1]
        ff = factors[:, 2 * layer + 1 : 2 * layer + 2]
        start, a, q, k, v, o, lse, mid, a2, gbs, slopes = saved[layer]
        eb = (ff * up).astype(BF)
        bias2 = jnp.sum(eb.astype(F32), axis=0, keepdims=True)
        dus = []
        dn = 0.0
        for part in range(4):
            du = (nn(eb, w2[part]) * slopes[part]).astype(BF)
            dus.append(du)
            dn = dn + nt(du, w1[part])
        first_bias = [jnp.sum(du.astype(F32), axis=0, keepdims=True) for du in dus]
        du_x = jnp.where(s_high == 0, dus[0], dus[2])
        du_y = jnp.where(s_low == 0, dus[1], dus[3])
        gb_x = jnp.where(s_high == 0, gbs[0], gbs[2])
        gb_y = jnp.where(s_low == 0, gbs[1], gbs[3])
        _, scaled, inverse = normalize(mid, vec[5], vec[6])
        gain2 = jnp.sum(dn * scaled, axis=0, keepdims=True)
        shift2 = jnp.sum(dn, axis=0, keepdims=True)
        up = (up + normalize_back(dn, scaled, inverse, vec[5])).astype(BF).astype(F32)
        feed_rows, feed = reduced(
            [(tn(a2, du_x), tn(a2, du_y)), (tn(eb, gb_x), tn(eb, gb_y))],
            [gain2, shift2, bias2] + first_bias,
        )

        eb = (fa * up).astype(BF)
        out_bias = jnp.sum(eb.astype(F32), axis=0, keepdims=True)
        do = nt(eb, wa[3]).astype(BF)
        dq, dk, dv = attention_back(q, k, v, do, lse, code_q, code_k)
        dn = nt(dq, wa[0]) + nt(dk, wa[1]) + nt(dv, wa[2])
        query_bias = jnp.sum(dq.astype(F32), axis=0, keepdims=True)
        value_bias = jnp.sum(dv.astype(F32), axis=0, keepdims=True)
        _, scaled, inverse = normalize(start, vec[0], vec[1])
        gain1 = jnp.sum(dn * scaled, axis=0, keepdims=True)
        shift1 = jnp.sum(dn, axis=0, keepdims=True)
        up = up + normalize_back(dn, scaled, inverse, vec[0])
        if layer > 0:
            up = up.astype(BF).astype(F32)
        grad_x = tn(a, jnp.where(s_high == 0, dq, dv))
        grad_y = tn(jnp.where(s_low == 0, a, o), jnp.where(s_low == 0, dk, eb))
        attention_rows, done = reduced(
            [(grad_x, grad_y)], [gain1, shift1, query_bias, value_bias, out_bias]
        )
        attention_grads[layer] = done[0]
        feed_grads[layer] = jnp.stack(feed)
        vector_grads[layer] = jnp.concatenate([attention_rows, feed_rows])

    def outward(rows):
        blocks = [rows[:, i * (width // 4) : (i + 1) * (width // 4)] for i in range(4)]
        mine = pick(s, blocks)
        theirs = lax.ppermute(pick(s ^ 1, blocks), "section", across)
        return jnp.where(unit == 0, jnp.stack([mine, theirs]), jnp.stack([theirs, mine]))

    block_result = outward(hidden.astype(BF))
    input_result = outward(up.astype(BF)).astype(F32)

    vector_grad = jnp.stack(vector_grads)
    attention_grad = jnp.stack(attention_grads)
    feedforward_grad = jnp.stack(feed_grads)
    vector_mean, vector_square, vector_step = adam_update(
        vector_params, vector_first, vector_second, vector_grad, layer_rates, 0.0
    )
    attention_mean, attention_square, attention_step = adam_update(
        attention_weights,
        attention_first,
        attention_second,
        attention_grad,
        layer_rates,
        decay_rate,
    )
    feedforward_mean, feedforward_square, feedforward_step = adam_update(
        feedforward_weights,
        feedforward_first,
        feedforward_second,
        feedforward_grad,
        layer_rates,
        decay_rate,
    )
    return (
        block_result,
        input_result,
        vector_grad,
        attention_grad,
        feedforward_grad,
        vector_mean,
        attention_mean,
        feedforward_mean,
        vector_square,
        attention_square,
        feedforward_square,
        vector_step,
        attention_step,
        feedforward_step,
    )


def solution(mesh):
    in_specs = (
        P(None, "dp", None),
        P(),
        P(None, "dp", None),
        P(None, "dp", None, None),
        P(None, "dp", None),
        P(None, None, "dp"),
        P(None, "dp", None),
        P(None, None, "dp", None),
        P(None, None, "dp"),
        P(None, "dp", None),
        P(None, None, "dp", None),
        P(None, None, "dp"),
        P(None, "dp", None),
        P(None, None, "dp", None),
        P(),
    )
    out_specs = (
        P(None, "dp", "section"),
        P(None, "dp", "section"),
        P(None, None, "dp"),
        P(None, "dp", None),
        P(None, None, "dp", None),
        P(None, None, "dp"),
        P(None, "dp", None),
        P(None, None, "dp", None),
        P(None, None, "dp"),
        P(None, "dp", None),
        P(None, None, "dp", None),
        P(None, None, "dp"),
        P(None, "dp", None),
        P(None, None, "dp", None),
    )
    return jax.shard_map(shards, mesh=mesh, in_specs=in_specs, out_specs=out_specs, check_vma=False)
```

time: 1650 us -> 653 us (0.40)
  waiting for transfers between devices: 991 us -> 137 us
  loops' own time: 86.7 us -> 0 us
  Pallas kernels: 0 us -> 85.6 us
  matrix products: 203 us -> 129 us
  other arithmetic: 134 us -> 67.4 us
  starting transfers between devices: 22.8 us -> 64.6 us
  blocking collectives: 49.3 us -> 21.9 us
  local copies, waits for them, and re-layouts: 139 us -> 119 us
    ppermute x8 -> x63, waiting for transfers between devices: 375 us -> 94.8 us  [the longest x8 50.8 us: reduced(): other = lax.ppermute(jnp.concatenate(other, axis=1), 'section', route)]
    reduce_scatter x2 -> x0, waiting for transfers between devices: 243 us -> none  [the longest x1 186 us: shards(): lax.psum_scatter(feedforward_total, 'dp', scatter_dimension=1, tiled=True)]
    psum x1 -> x0, waiting for transfers between devices: 151 us -> none  [shards(): lax.psum((place_layer(vector_sum, layer_id, layer_total), place_layer(att...]
    unnamed x11 -> x10, waiting for transfers between devices: 112 us -> 0.16 us
    another operation x10 -> x0, loops' own time: 86.7 us -> none  [the longest x5 48.5 us: shards(): lax.switch(branch_pick, (spare_backward, attention_back_run, feedforward_...]
    pallas_call x0 -> x8, Pallas kernels: none -> 85.6 us  [the longest x2 36.9 us: attention_back(): pl.pallas_call(attention_back_kernel, grid=(width // (2 * HD),), in_specs...]
    all_gather x4 -> x2, waiting for transfers between devices: 110 us -> 41.8 us  [reduced(): everyone = lax.all_gather(everyone, 'section', axis=0, tiled=False)]
    sub x4 -> x0, matrix products: 48.1 us -> none  [attention_parts(): exp_scores = jnp.exp(scores - row_peak)]
  transfers between devices with their start and end apart: 17 -> 69, of which waited for: 14 -> 23; matrix products, arithmetic and copies ran while one was open for 11% -> 29% of each run, Pallas kernels for 0% -> 7%
where the time goes in v1:
time: 653 us; the launch traced here: 642 us
  waiting for transfers between devices  137 us (21%)
  matrix products  129 us (20%)
  local copies, waits for them, and re-layouts  119 us (18%)
  Pallas kernels  85.6 us (13%)
  other arithmetic  67.4 us (10%)
  starting transfers between devices  64.6 us (10%)
  blocking collectives  21.9 us (3%)
  between operations  17.9 us (3%)
    unnamed x475, local copies, waits for them, and re-layouts  55.5 us
    dot_general x24, matrix products, nt(): lax.dot_general(a, b, (((1,), (1,)), ((), ())), preferred_element_type=F32)  53.5 us
    ppermute x8, waiting for transfers between devices, reduced(): other = lax.ppermute(jnp.concatenate(other, axis=1), 'section', route)  50.8 us
    dot_general x24, matrix products, nn(): return jnp.dot(a, b, preferred_element_type=F32)  49.3 us
    all_gather x2, waiting for transfers between devices, reduced(): everyone = lax.all_gather(everyone, 'section', axis=0, tiled=False)  41.8 us
    pallas_call x2, Pallas kernels, attention_back(): pl.pallas_call(attention_back_kernel, grid=(width // (2 * HD),), in_specs...  36.9 us
    ppermute x12, starting transfers between devices, shards(): far = [lax.ppermute(sent, 'dp', route) for route in around]  26.7 us
    pallas_call x2, Pallas kernels, attention(): pl.pallas_call(attention_kernel, grid=(width // (2 * HD),), in_specs=[pai...  26.1 us
  transfers between devices with their start and end apart: 69, of which 23 were waited for; matrix products, arithmetic and copies ran while one was open for 29% of the time, Pallas kernels for 7%

profile of v1, /device:TPU:0, one launch (start us, length us, event | category | flops | bytes accessed | tf_op | source)
XLA Modules:
  0.0 642.0 jit_solution(2095022523181945713)
XLA Ops:
  10.8 5.0 collective-permute-start.2
  62.8 8.8 %collective-permute-start.41 = (bf16[192,768]{1,0:T(8,128)(2,1)S(1)}, bf16[192,768]{1,0:T(8,128)(2,1)S(1)}, u32[]{:S(2)}, u32[]{:S(2)}) collective-permute-start(bf16[192,768]{1,0:T(8,128)(2,1)S(1)} %bitcast.524), channel_id=1, source_target_pairs={{0,2},{1,3},{2,4},{3,5},{4,6},{5,7},{6,0},{7,1},{8,10},{9,11},{10,... | collective-permute-start | bytes 884744 | tf_op jit(solution)/shard_map/ppermute | solution.py:276
  86.2 8.9 %collective-permute-done.42 = bf16[192,768]{1,0:T(8,128)(2,1)S(1)} collective-permute-done((bf16[192,768]{1,0:T(8,128)(2,1)S(1)}, bf16[192,768]{1,0:T(8,128)(2,1)S(1)}, u32[]{:S(2)}, u32[]{:S(2)}) %collective-permute-start.42) | collective-permute-done | bytes 294944 | tf_op jit(solution)/shard_map/ppermute | solution.py:276
  101.9 5.9 collective-permute-done.8.refs_6_
  119.3 4.6 collective-permute-done.10.refs_8_
  142.7 5.0 assemble.4
  155.5 13.1 %attention.2 = (bf16[640,768]{1,0:T(8,128)(2,1)S(1)}, f32[6,640,2]{2,1,0:T(8,128)S(1)}) custom-call(bf16[640,768]{1,0:T(8,128)(2,1)S(1)} %add_convert_fusion.9.q_ref, bf16[640,768]{1,0:T(8,128)(2,1)S(1)} %convolution_convert_fusion.15.k_ref, bf16[640,768]{1,0:T(8,128)(2,1)S(1)} %add_convert_fusion.8.v_ref, ...), custom_call_target="tpu_custom_call" | custom-call | tf_op jit(solution)/shard_map/attention/pallas_call | solution.py:140
  172.8 5.1 collective-permute-done.23.refs_8_
  185.7 8.8 %assemble.5 = bf16[2,4,768,768]{3,2,1,0:T(8,128)(2,1)S(1)} custom-call(s32[3]{0:T(128)S(1)} %pad_add_fusion.at_ref, bf16[2,4,96,768]{3,2,1,0:T(8,128)(2,1)} %pad_maximum_fusion.8.refs_0_, bf16[2,4,96,768]{3,2,1,0:T(8,128)(2,1)} %collective-permute-done.14.refs_1_, bf16[3,2,96,768]{3,2,1,0:T(8,128)(2,1)S(1)} %copy-done.18, ...), custom_call_target="tpu_custom_call" | custom-call | tf_op jit(solution)/shard_map/assemble/pallas_call | solution.py:200
  216.4 13.1 %attention.3 = (bf16[640,768]{1,0:T(8,128)(2,1)S(1)}, f32[6,640,2]{2,1,0:T(8,128)S(1)}) custom-call(bf16[640,768]{1,0:T(8,128)(2,1)S(1)} %add_convert_fusion.6.q_ref, bf16[640,768]{1,0:T(8,128)(2,1)S(1)} %copy-done.15, bf16[640,768]{1,0:T(8,128)(2,1)S(1)} %copy-done.11, bf16[640,128]{1,0:T(8,128)(2,1)S(1)} %compare_convert_fusion.code_q_ref, ...), custom_call_target="tpu_custom_call" | custom-call | tf_op jit(solution)/shard_map/attention/pallas_call | solution.py:140
  269.0 18.4 %attention_back.2 = (bf16[640,768]{1,0:T(8,128)(2,1)S(1)}, bf16[640,768]{1,0:T(8,128)(2,1)S(1)}, bf16[640,768]{1,0:T(8,128)(2,1)S(1)}) custom-call(bf16[640,768]{1,0:T(8,128)(2,1)S(1)} %copy-done.14, bf16[640,768]{1,0:T(8,128)(2,1)S(1)} %copy-done.16, bf16[640,768]{1,0:T(8,128)(2,1)S(1)} %copy-done.12, bf16[640,768]{1,0:T(8,128)(2,1)} %convolution_convert_fusion.13.do_ref, ...), custom_call_target="tpu_custom_call" | custom-call | tf_op jit(solution)/shard_map/attention_back/pallas_call | solution.py:158
  319.6 18.4 %attention_back.3 = (bf16[640,768]{1,0:T(8,128)(2,1)S(1)}, bf16[640,768]{1,0:T(8,128)(2,1)S(1)}, bf16[640,768]{1,0:T(8,128)(2,1)S(1)}) custom-call(bf16[640,768]{1,0:T(8,128)(2,1)S(1)} %copy-done.8, bf16[640,768]{1,0:T(8,128)(2,1)S(1)} %copy-done.10, bf16[640,768]{1,0:T(8,128)(2,1)S(1)} %copy-done.6, bf16[640,768]{1,0:T(8,128)(2,1)} %convolution_convert_fusion.12.do_ref, ...), custom_call_target="tpu_custom_call" | custom-call | tf_op jit(solution)/shard_map/attention_back/pallas_call | solution.py:158
  347.7 4.6 convolution_convert_fusion.11
  372.9 10.0 %collective-permute-done.56 = bf16[768,384]{0,1:T(8,128)(2,1)} collective-permute-done((bf16[768,384]{0,1:T(8,128)(2,1)}, bf16[768,384]{0,1:T(8,128)(2,1)}, u32[]{:S(2)}, u32[]{:S(2)}) %collective-permute-start.56) | collective-permute-done | bytes 589856 | tf_op jit(solution)/shard_map/ppermute | solution.py:365
  420.4 19.4 %collective-permute-done.58 = bf16[768,768]{0,1:T(8,128)(2,1)} collective-permute-done((bf16[768,768]{0,1:T(8,128)(2,1)}, bf16[768,768]{0,1:T(8,128)(2,1)}, u32[]{:S(2)}, u32[]{:S(2)}) %collective-permute-start.58) | collective-permute-done | bytes 1179680 | tf_op jit(solution)/shard_map/ppermute | solution.py:365
  441.5 8.5 %collective-permute-done.57 = bf16[768,896]{0,1:T(8,128)(2,1)} collective-permute-done((bf16[768,896]{0,1:T(8,128)(2,1)}, bf16[768,896]{0,1:T(8,128)(2,1)}, u32[]{:S(2)}, u32[]{:S(2)}) %collective-permute-start.57) | collective-permute-done | bytes 1376288 | tf_op jit(solution)/shard_map/ppermute | solution.py:365
  485.9 10.4 %collective-permute-done.62 = bf16[768,768]{0,1:T(8,128)(2,1)S(1)} collective-permute-done((bf16[768,768]{0,1:T(8,128)(2,1)S(1)}, bf16[768,768]{0,1:T(8,128)(2,1)S(1)}, u32[]{:S(2)}, u32[]{:S(2)}) %collective-permute-start.62) | collective-permute-done | bytes 1179680 | tf_op jit(solution)/shard_map/ppermute | solution.py:365
  503.9 5.0 fusion.60
  518.9 12.5 %all-gather = bf16[384,768]{1,0:T(8,128)(2,1)S(1)} all-gather(bf16[96,768]{1,0:T(8,128)(2,1)S(1)} %copy.1114), channel_id=2, replica_groups=mesh['section'=4,'dp'=8] {'section'}, dimensions={0}, use_global_device_ids=true | all-gather | bytes 737280 | tf_op jit(solution)/shard_map/all_gather | solution.py:372
  533.0 9.4 %all-gather.1 = bf16[384,768]{1,0:T(8,128)(2,1)S(1)} all-gather(bf16[96,768]{1,0:T(8,128)(2,1)S(1)} %copy.1115), channel_id=3, replica_groups=mesh['section'=4,'dp'=8] {'section'}, dimensions={0}, use_global_device_ids=true | all-gather | bytes 737280 | tf_op jit(solution)/shard_map/all_gather | solution.py:372
  549.7 7.6 %add_multiply_fusion.1 = (f32[2,96,3072]{2,1,0:T(8,128)}, f32[2,96,3072]{2,1,0:T(8,128)}, f32[2,96,3072]{2,1,0:T(8,128)}, f32[2,96,3072]{2,1,0:T(8,128)}) fusion(f32[2,96,3072]{2,1,0:T(8,128)} %param.21, f32[2]{0:T(128)S(1)} %copy-done.139, f32[2,96,3072]{2,1,0:T(8,128)} %param.27, f32[2,96,3072]{2,1,0:T(8,128)} %param.24, ...), kind=kLoop, calls=%fused_computation.41 | loop fusion | flops 9437184 | bytes 17694728 | tf_op jit(solution)/shard_map/mul | solution.py:215
  560.3 17.6 %all-gather.7.cloned.1.call-done = bf16[384,1536]{1,0:T(8,128)(2,1)} async-done(((bf16[96,1536]{1,0:T(8,128)(2,1)}), bf16[384,1536]{1,0:T(8,128)(2,1)}) %all-gather.7.cloned.1.call-update) | async-done | bytes 1179664 | tf_op jit(solution)/shard_map/all_gather | solution.py:372
  583.7 24.2 %all-gather.9.cloned.1.call-done = bf16[384,1536]{1,0:T(8,128)(2,1)} async-done(((bf16[96,1536]{1,0:T(8,128)(2,1)}), bf16[384,1536]{1,0:T(8,128)(2,1)}) %all-gather.9.cloned.1.call-update) | async-done | bytes 1179664 | tf_op jit(solution)/shard_map/all_gather | solution.py:372
  624.6 10.1 %add_multiply_fusion = (f32[2,2,96,3072]{3,2,1,0:T(8,128)}, f32[2,2,96,3072]{3,2,1,0:T(8,128)}, f32[2,2,96,3072]{3,2,1,0:T(8,128)}, f32[2,2,96,3072]{3,2,1,0:T(8,128)}) fusion(f32[2,2,96,3072]{3,2,1,0:T(8,128)S(1)} %bitcast.514, f32[2]{0:T(128)S(1)} %copy-done.139, f32[2,2,96,3072]{3,2,1,0:T(8,128)S(1)} %bitcast.516, f32[2,2,96,3072]{3,2,1,0:T(8,128)} %param.25, ...), kind=kLoop, calls=%fused_computation.3 | loop fusion | flops 18874368 | bytes 35389448 | tf_op jit(solution)/shard_map/mul | solution.py:215
  (882 shorter events, 369.6 us)
Async XLA Ops:
  7.2 510.3 %reduce-scatter.13.cloned.1.call-start = ((), (), s32[]{:S(2)}) async-start(), calls=%async_computation.6 | async-start | bytes 1548288
  10.8 37.1 %collective-permute-start.2 = (bf16[112,768]{1,0:T(8,128)(2,1)}, bf16[112,768]{1,0:T(8,128)(2,1)}, u32[]{:S(2)}, u32[]{:S(2)}) collective-permute-start(bf16[112,768]{1,0:T(8,128)(2,1)} %pad_maximum_fusion.24), channel_id=1, source_target_pairs={{0,6},{1,7},{2,0},{3,1},{4,2},{5,3},{6,4},{7,5},{8,14},{9,15},{10,... | collective-permute-start | bytes 516104 | tf_op jit(solution)/shard_map/ppermute | solution.py:276
  15.9 33.8 %collective-permute-start.1 = (bf16[112,768]{1,0:T(8,128)(2,1)}, bf16[112,768]{1,0:T(8,128)(2,1)}, u32[]{:S(2)}, u32[]{:S(2)}) collective-permute-start(bf16[112,768]{1,0:T(8,128)(2,1)} %pad_maximum_fusion.24), channel_id=1, source_target_pairs={{0,4},{1,5},{2,6},{3,7},{4,0},{5,1},{6,2},{7,3},{8,12},{9,13},{10,... | collective-permute-start | bytes 516104 | tf_op jit(solution)/shard_map/ppermute | solution.py:276
  15.9 35.6 %collective-permute-start = (bf16[112,768]{1,0:T(8,128)(2,1)}, bf16[112,768]{1,0:T(8,128)(2,1)}, u32[]{:S(2)}, u32[]{:S(2)}) collective-permute-start(bf16[112,768]{1,0:T(8,128)(2,1)} %pad_maximum_fusion.24), channel_id=1, source_target_pairs={{0,2},{1,3},{2,4},{3,5},{4,6},{5,7},{6,0},{7,1},{8,10},{9,11},{10,... | collective-permute-start | bytes 516104 | tf_op jit(solution)/shard_map/ppermute | solution.py:276
  21.3 52.2 %collective-permute-start.15 = (bf16[192,768]{1,0:T(8,128)(2,1)}, bf16[192,768]{1,0:T(8,128)(2,1)}, u32[]{:S(2)}, u32[]{:S(2)}) collective-permute-start(bf16[192,768]{1,0:T(8,128)(2,1)} %bitcast.36), channel_id=1, source_target_pairs={{0,2},{1,3},{2,4},{3,5},{4,6},{5,7},{6,0},{7,1},{8,10},{9,11},{10,... | collective-permute-start | bytes 884744 | tf_op jit(solution)/shard_map/ppermute | solution.py:276
  23.7 53.2 %collective-permute-start.16 = (bf16[192,768]{1,0:T(8,128)(2,1)}, bf16[192,768]{1,0:T(8,128)(2,1)}, u32[]{:S(2)}, u32[]{:S(2)}) collective-permute-start(bf16[192,768]{1,0:T(8,128)(2,1)} %bitcast.36), channel_id=1, source_target_pairs={{0,4},{1,5},{2,6},{3,7},{4,0},{5,1},{6,2},{7,3},{8,12},{9,13},{10,... | collective-permute-start | bytes 884744 | tf_op jit(solution)/shard_map/ppermute | solution.py:276
  60.7 36.1 %collective-permute-start.4 = (bf16[1,4,96,768]{3,2,1,0:T(8,128)(2,1)S(1)}, bf16[1,4,96,768]{3,2,1,0:T(8,128)(2,1)S(1)}, u32[]{:S(2)}, u32[]{:S(2)}) collective-permute-start(bf16[1,4,96,768]{3,2,1,0:T(8,128)(2,1)S(1)} %bitcast.509), channel_id=1, source_target_pairs={{0,1},{1,0},{2,3},{3,2},{4,5},{5,4},{6,7},{7,6},{8,9},{9,8},{10,11... | collective-permute-start | bytes 1769480 | tf_op jit(solution)/shard_map/ppermute | solution.py:287
  140.6 28.0 %collective-permute-start.47 = (bf16[3,2,96,768]{3,2,1,0:T(8,128)(2,1)}, bf16[3,2,96,768]{3,2,1,0:T(8,128)(2,1)}, u32[]{:S(2)}, u32[]{:S(2)}) collective-permute-start(bf16[3,2,96,768]{3,2,1,0:T(8,128)(2,1)} %pad_maximum_fusion.17.refs_2_), channel_id=1, source_target_pairs={{0,16},{8,24},{16,0},{24,8},{1,17},{9,25},{17,1},{25,9},{2,18},{10... | collective-permute-start | bytes 2654216 | tf_op jit(solution)/shard_map/ppermute | solution.py:282
  141.6 28.3 %collective-permute-start.45 = (bf16[3,2,96,768]{3,2,1,0:T(8,128)(2,1)}, bf16[3,2,96,768]{3,2,1,0:T(8,128)(2,1)}, u32[]{:S(2)}, u32[]{:S(2)}) collective-permute-start(bf16[3,2,96,768]{3,2,1,0:T(8,128)(2,1)} %pad_maximum_fusion.17.refs_2_), channel_id=1, source_target_pairs={{0,8},{8,0},{16,24},{24,16},{1,9},{9,1},{17,25},{25,17},{2,10},{10... | collective-permute-start | bytes 2654216 | tf_op jit(solution)/shard_map/ppermute | solution.py:281
  149.6 33.0 %collective-permute-start.14 = (bf16[2,4,96,768]{3,2,1,0:T(8,128)(2,1)}, bf16[2,4,96,768]{3,2,1,0:T(8,128)(2,1)}, u32[]{:S(2)}, u32[]{:S(2)}) collective-permute-start(bf16[2,4,96,768]{3,2,1,0:T(8,128)(2,1)} %pad_maximum_fusion.8.refs_0_), channel_id=1, source_target_pairs={{0,1},{1,0},{2,3},{3,2},{4,5},{5,4},{6,7},{7,6},{8,9},{9,8},{10,11... | collective-permute-start | bytes 3538952 | tf_op jit(solution)/shard_map/ppermute | solution.py:287
  182.6 51.7 %collective-permute-start.40 = (bf16[2,4,96,768]{3,2,1,0:T(8,128)(2,1)}, bf16[2,4,96,768]{3,2,1,0:T(8,128)(2,1)}, u32[]{:S(2)}, u32[]{:S(2)}) collective-permute-start(bf16[2,4,96,768]{3,2,1,0:T(8,128)(2,1)} %pad_maximum_fusion.9.refs_0_), channel_id=1, source_target_pairs={{0,1},{1,0},{2,3},{3,2},{4,5},{5,4},{6,7},{7,6},{8,9},{9,8},{10,11... | collective-permute-start | bytes 3538952 | tf_op jit(solution)/shard_map/ppermute | solution.py:287
  182.7 46.8 %collective-permute-start.44 = (bf16[3,2,96,768]{3,2,1,0:T(8,128)(2,1)}, bf16[3,2,96,768]{3,2,1,0:T(8,128)(2,1)S(1)}, u32[]{:S(2)}, u32[]{:S(2)}) collective-permute-start(bf16[3,2,96,768]{3,2,1,0:T(8,128)(2,1)} %pad_maximum_fusion.17.refs_2_), channel_id=1, source_target_pairs={{0,1},{1,0},{2,3},{3,2},{4,5},{5,4},{6,7},{7,6},{8,9},{9,8},{10,11... | collective-permute-start | bytes 2654216 | tf_op jit(solution)/shard_map/ppermute | solution.py:287
  183.1 50.0 %collective-permute-start.49 = (bf16[3,2,96,384]{3,2,1,0:T(8,128)(2,1)}, bf16[3,2,96,384]{3,2,1,0:T(8,128)(2,1)}, u32[]{:S(2)}, u32[]{:S(2)}) collective-permute-start(bf16[3,2,96,384]{3,2,1,0:T(8,128)(2,1)} %slice.695), channel_id=1, source_target_pairs={{0,8},{8,0},{16,24},{24,16},{1,9},{9,1},{17,25},{25,17},{2,10},{10... | collective-permute-start | bytes 1327112 | tf_op jit(solution)/shard_map/ppermute | solution.py:283
  183.8 49.9 %collective-permute-start.51 = (bf16[3,2,96,384]{3,2,1,0:T(8,128)(2,1)}, bf16[3,2,96,384]{3,2,1,0:T(8,128)(2,1)}, u32[]{:S(2)}, u32[]{:S(2)}) collective-permute-start(bf16[3,2,96,384]{3,2,1,0:T(8,128)(2,1)} %slice.696), channel_id=1, source_target_pairs={{0,16},{8,24},{16,0},{24,8},{1,17},{9,25},{17,1},{25,9},{2,18},{10... | collective-permute-start | bytes 1327112 | tf_op jit(solution)/shard_map/ppermute | solution.py:284
  184.6 51.4 %collective-permute-start.46 = (bf16[3,2,96,768]{3,2,1,0:T(8,128)(2,1)}, bf16[3,2,96,768]{3,2,1,0:T(8,128)(2,1)}, u32[]{:S(2)}, u32[]{:S(2)}) collective-permute-start(bf16[3,2,96,768]{3,2,1,0:T(8,128)(2,1)} %collective-permute-done.45.refs_4_), channel_id=1, source_target_pairs={{0,1},{1,0},{2,3},{3,2},{4,5},{5,4},{6,7},{7,6},{8,9},{9,8},{10,11... | collective-permute-start | bytes 2654216 | tf_op jit(solution)/shard_map/ppermute | solution.py:287
  372.2 37.9 %collective-permute-start.59 = (bf16[768,512]{0,1:T(8,128)(2,1)}, bf16[768,512]{0,1:T(8,128)(2,1)}, u32[]{:S(2)}, u32[]{:S(2)}) collective-permute-start(bf16[768,512]{0,1:T(8,128)(2,1)} %pad_maximum_fusion.14), channel_id=1, source_target_pairs={{0,8},{8,0},{16,24},{24,16},{1,9},{9,1},{17,25},{25,17},{2,10},{10... | collective-permute-start | bytes 2359304 | tf_op jit(solution)/shard_map/ppermute | solution.py:365
  389.3 142.3 %reduce-scatter.17.cloned.1.call-start = ((), (), s32[]{:S(2)}) async-start(), calls=%async_computation.8 | async-start | bytes 1548288
  413.2 131.2 %reduce-scatter.15.cloned.1.call-start = ((), (), s32[]{:S(2)}) async-start(), calls=%async_computation.7 | async-start | bytes 2875392
  419.6 30.5 %collective-permute-start.57 = (bf16[768,896]{0,1:T(8,128)(2,1)}, bf16[768,896]{0,1:T(8,128)(2,1)}, u32[]{:S(2)}, u32[]{:S(2)}) collective-permute-start(bf16[768,896]{0,1:T(8,128)(2,1)} %pad_maximum_fusion.2), channel_id=1, source_target_pairs={{0,8},{8,0},{16,24},{24,16},{1,9},{9,1},{17,25},{25,17},{2,10},{10... | collective-permute-start | bytes 4128776 | tf_op jit(solution)/shard_map/ppermute | solution.py:365
  458.0 89.3 %reduce-scatter.19.cloned.1.call-start = ((), (), s32[]{:S(2)}) async-start(), calls=%async_computation.9 | async-start | bytes 2875392
  463.9 32.8 %collective-permute-start.61 = (bf16[768,896]{0,1:T(8,128)(2,1)S(1)}, bf16[768,896]{0,1:T(8,128)(2,1)S(1)}, u32[]{:S(2)}, u32[]{:S(2)}) collective-permute-start(bf16[768,896]{0,1:T(8,128)(2,1)S(1)} %pad_maximum_fusion.4), channel_id=1, source_target_pairs={{0,8},{8,0},{16,24},{24,16},{1,9},{9,1},{17,25},{25,17},{2,10},{10... | collective-permute-start | bytes 4128776 | tf_op jit(solution)/shard_map/ppermute | solution.py:365
  474.4 35.9 %collective-permute-start.54 = (bf16[640,192]{1,0:T(8,128)(2,1)S(1)}, bf16[640,192]{1,0:T(8,128)(2,1)}, u32[]{:S(2)}, u32[]{:S(2)}) collective-permute-start(bf16[640,192]{1,0:T(8,128)(2,1)S(1)} %get-tuple-element.447), channel_id=1, source_target_pairs={{0,8},{8,0},{16,24},{24,16},{1,9},{9,1},{17,25},{25,17},{2,10},{10... | collective-permute-start | bytes 737288 | tf_op jit(solution)/shard_map/ppermute | solution.py:437
  503.2 74.6 %all-gather.7.cloned.1.call-start = ((), (), s32[]{:S(2)}) async-start(), calls=%async_computation.4 | async-start | bytes 1474560 | tf_op jit(solution)/shard_map/all_gather | solution.py:372
  546.8 61.1 %all-gather.9.cloned.1.call-start = ((), (), s32[]{:S(2)}) async-start(), calls=%async_computation.5 | async-start | bytes 1474560 | tf_op jit(solution)/shard_map/all_gather | solution.py:372
  (254 other events, 2760.9 us)
Sparse Core Ops, SparseCore 0:
  389.4 36.7 reduce-scatter.12
  429.2 31.5 reduce-scatter.16
  463.7 35.3 reduce-scatter.14
  503.4 41.6 reduce-scatter.18
  547.3 30.5 all-gather.6
  580.1 27.7 all-gather.8
